TPU v7x, 32 devices: a whole 2x2x4 slice. The times are simulated.
32 devices in a mesh: freq: 4 (over x, core), facet: 8 (over z, y).
Axes of the slice: x: 2, y: 2, z: 4, core: 2. Of those that a mesh axis runs over, the one named last changes fastest.
Arguments:
- visibilities: float32 [16, 2, 2048], P('facet', None, 'freq'), may hold values from -6 to 6
- weights: float32 [16, 2048], P('facet', 'freq'), may hold values from 0.1 to 1
- uv_cells: int32 [16, 2, 2048], P('facet', None, 'freq'), may hold values from -16384 to 16383
- flags: int32 [16, 2048], P('facet', 'freq'), may hold values from 0 to 1, as said below
- plan: int32 [16], replicated, may hold values from 0 to 15, each once
- beam: float32 [8, 16], P('facet'), may hold values from 0.2 to 1
- facets: int32 [8, 2], P('facet'), may hold values from 0 to 255
Outputs:
- dirty_image: float32 [8, 128, 128], P('facet', 'freq')
Inputs may be any that keep to these rules, and one draw needn't show every extreme that they name: `flags`: in each block, each frequency group's 512 rows hold at most 256 unflagged rows; in every draw some block holds exactly 256 in every group. `plan`: each of the 16 blocks is read at exactly one step.
All inputs are finite; a program needn't handle non-finite values.
Results may differ from a plain program's by a relative error of at most 0.0037.
Values sent between devices are 32-bit elements; how exact they have to be, the bound alone decides.
A program may use at most 64 MiB of HBM per device.

v0:
```python
import math

import jax
import jax.numpy as jnp
from jax import lax
from jax.sharding import PartitionSpec as P

P_SIZE = 128
IMG = 32768


full_turn = 2.0 * math.pi
slab_limit = 16384
fine_count = 16


def angle_table(factors, cells):
    turns = jnp.mod(factors[:, None] * cells[None, :], IMG).astype(jnp.float32) * (full_turn / IMG)
    return (jnp.cos(turns), jnp.sin(turns))


def phase_table(base, cells):
    coarse_count = P_SIZE // fine_count
    base_cos, base_sin = angle_table(jnp.reshape(base, (1,)), cells)
    coarse_cos, coarse_sin = angle_table(
        jnp.arange(coarse_count, dtype=jnp.int32) * fine_count, cells
    )
    fine_cos, fine_sin = angle_table(jnp.arange(fine_count, dtype=jnp.int32), cells)
    outer_cos = base_cos * coarse_cos - base_sin * coarse_sin
    outer_sin = base_sin * coarse_cos + base_cos * coarse_sin
    full_cos = (
        outer_cos[:, None, :] * fine_cos[None, :, :] - outer_sin[:, None, :] * fine_sin[None, :, :]
    )
    full_sin = (
        outer_sin[:, None, :] * fine_cos[None, :, :] + outer_cos[:, None, :] * fine_sin[None, :, :]
    )
    extent = cells.shape[0]
    return (full_cos.reshape(P_SIZE, extent), full_sin.reshape(P_SIZE, extent))


def facet_image(samples, facet_col, facet_row):
    u_cells = samples[3].astype(jnp.int32)
    v_cells = samples[4].astype(jnp.int32)
    cos_u, sin_u = phase_table(facet_col * P_SIZE - IMG // 2, u_cells)
    real_part = samples[0] * samples[2]
    imag_part = samples[1] * samples[2]
    left = jnp.concatenate(
        [real_part * cos_u - imag_part * sin_u, -(real_part * sin_u + imag_part * cos_u)], axis=1
    ).astype(jnp.bfloat16)
    cos_v, sin_v = phase_table(facet_row * P_SIZE - IMG // 2, v_cells)
    right = jnp.concatenate([cos_v, sin_v], axis=1).astype(jnp.bfloat16)
    return lax.dot_general(
        left, right, (((1,), (1,)), ((), ())), preferred_element_type=jnp.float32
    )


def slab_image(samples, facet_col, facet_row):
    extent = samples.shape[1]
    if extent > slab_limit and extent % slab_limit == 0:
        slabs = samples.reshape(5, extent // slab_limit, slab_limit).transpose(1, 0, 2)

        def advance(running, slab):
            return (running + facet_image(slab, facet_col, facet_row), None)

        summed, _ = lax.scan(advance, jnp.zeros((P_SIZE, P_SIZE), jnp.float32), slabs)
        return summed
    return facet_image(samples, facet_col, facet_row)


def flatten_blocks(packed, factors):
    scaled = packed[:, 2, :] * factors[:, None]
    joined = jnp.concatenate([packed[:, :2, :], scaled[:, None, :], packed[:, 3:, :]], axis=1)
    return joined.transpose(1, 0, 2).reshape(5, -1)


def body(visibilities, weights, uv_cells, flags, plan, beam, facets):
    live = weights * flags.astype(jnp.float32)
    packed = jnp.concatenate([visibilities, live[:, None, :], uv_cells.astype(jnp.float32)], axis=1)
    total_blocks = plan.shape[0]
    matches = (plan[:, None] == jnp.arange(total_blocks, dtype=jnp.int32)[None, :]).astype(
        jnp.float32
    )
    gains = jnp.sum(beam[0][:, None] * matches, axis=0)
    facet_col = facets[0, 0]
    facet_row = facets[0, 1]
    image = slab_image(
        flatten_blocks(lax.all_gather(packed, "facet", axis=0, tiled=True), gains),
        facet_col,
        facet_row,
    )
    share = lax.psum_scatter(image, "freq", scatter_dimension=0, tiled=True)
    scale = 2.0 / math.sqrt(total_blocks * weights.shape[1] * lax.axis_size("freq"))
    return (share * scale)[None]


def solution(mesh):
    in_specs = (
        P("facet", None, "freq"),
        P("facet", "freq"),
        P("facet", None, "freq"),
        P("facet", "freq"),
        P(),
        P("facet", None),
        P("facet", None),
    )
    out_specs = P("facet", "freq", None)
    return jax.shard_map(body, mesh=mesh, in_specs=in_specs, out_specs=out_specs, check_vma=False)
```

profile of v0, /device:TPU:0, one launch (start us, length us, event | category | flops | bytes accessed | tf_op | source)
XLA Modules:
  0.0 85.3 jit_solution(17814212700617278355)
XLA Ops:
  6.5 0.0 reduce-scatter.2.cloned.1.call-start
  6.5 1.3 %fusion.50 = (s32[1,1]{1,0:T(1,128)}, s32[1,1]{1,0:T(1,128)}) fusion(s32[1,2]{1,0:T(1,128)} %param.13), kind=kLoop, calls=%fused_computation.96 | loop fusion | bytes 16 | tf_op jit(solution)/shard_map/slice | solution.py:85
  9.1 0.7 convert_multiply_fusion
  9.8 0.7 convert_element_type.104
  10.5 0.7 pad_maximum_fusion
  11.2 32.5 %all_gather.3 = f32[16,5,512]{2,1,0:T(8,128)S(1)} all-gather(f32[2,5,512]{2,1,0:T(8,128)S(1)} %pad_maximum_fusion), channel_id=1, replica_groups=mesh['freq'=4,'facet'=8] {'facet'}, dimensions={0}, use_global_device_ids=true | all-gather | bytes 184320 | tf_op jit(solution)/shard_map/all_gather | solution.py:87
  43.7 0.1 fusion.49
  43.8 0.8 select_reduce_fusion
  44.5 0.1 slice_multiply_fusion.2
  44.6 0.1 maximum_bitcast_fusion
  44.7 0.1 slice_convert_fusion
  44.9 2.0 %fusion.31 = (f32[16,8192]{1,0:T(8,128)S(1)}, f32[16,8192]{1,0:T(8,128)S(1)}) fusion(s32[8192]{0:T(1024)S(1)} %bitcast.35), kind=kLoop, calls=%fused_computation.59 | loop fusion | flops 1835008 | bytes 1081344 | tf_op jit(solution)/shard_map/cos | solution.py:19
  46.9 0.1 fusion.45
  47.1 2.0 %fusion.33 = (f32[16,8192]{1,0:T(8,128)S(1)}, f32[16,8192]{1,0:T(8,128)S(1)}) fusion(s32[8192]{0:T(1024)S(1)} %bitcast.38), kind=kLoop, calls=%fused_computation.61 | loop fusion | flops 1835008 | bytes 1081344 | tf_op jit(solution)/shard_map/cos | solution.py:19
  49.1 0.1 fusion.47
  49.3 2.2 %multiply_subtract_fusion.1 = (f32[8,8192]{1,0:T(8,128)S(1)}, f32[8,8192]{1,0:T(8,128)S(1)}, f32[8,8192]{1,0:T(8,128)S(1)}, f32[8,8192]{1,0:T(8,128)S(1)}) fusion(f32[8192]{0:T(1024)S(1)} %get-tuple-element.24, f32[8192]{0:T(1024)S(1)} %get-tuple-element.23, s32[8192]{0:T(1024)S(1)} %bitcast.37, s32[8]{0:T(128)S(1)} %iota_multiply_fusion, ...), kind=kLoop, calls=%fused_computation.56 | loop fusion | flops 2621440 | bytes 1245216 | tf_op jit(solution)/shard_map/sub | solution.py:29
  51.5 2.1 %subtract_convert_fusion = (bf16[8,16,8192]{2,1,0:T(8,128)(2,1)S(1)}, bf16[8,16,8192]{2,1,0:T(8,128)(2,1)S(1)}, f32[8,16,8192]{2,1,0:T(8,128)S(1)}, f32[8,16,8192]{2,1,0:T(8,128)S(1)}) fusion(f32[16,8192]{1,0:T(8,128)S(1)} %get-tuple-element.22, f32[8,8192]{1,0:T(8,128)S(1)} %get-tuple-element.18, f32[16,8192]{1,0:T(8,128)S(1)} %get-tuple-element.21, ...), kind=kLoop, calls=%fused_computation.17 | loop fusion | flops 14680064 | bytes 15728640 | tf_op jit(solution)/shard_map/convert.3
  53.6 1.1 %fusion.8 = (bf16[128,8192]{1,0:T(8,128)(2,1)S(1)}, bf16[128,8192]{1,0:T(8,128)(2,1)S(1)}) fusion(f32[8,16,8192]{2,1,0:T(8,128)S(1)} %get-tuple-element.33, f32[8,16,8192]{2,1,0:T(8,128)S(1)} %get-tuple-element.34, f32[8192]{0:T(1024)S(1)} %bitcast.41, f32[8192]{0:T(1024)S(1)} %bitcast.42), kind=kLoop, calls=%fused_computation.10 | loop fusion | flops 9437184 | bytes 12648448 | tf_op jit(solution)/shard_map/convert.4
  54.7 1.9 %fusion = f32[128,128]{1,0:T(8,128)} fusion(bf16[128,8192]{1,0:T(8,128)(2,1)S(1)} %get-tuple-element.6, bf16[128,8192]{1,0:T(8,128)(2,1)S(1)} %get-tuple-element.5, bf16[128,8192]{1,0:T(8,128)(2,1)S(1)} %bitcast.34, bf16[128,8192]{1,0:T(8,128)(2,1)S(1)} %bitcast.33), kind=kOutput, calls=%fused_computation | convolution fusion | flops 553648128 | bytes 8454144 | tf_op jit(solution)/shard_map/dot_general | solution.py:52
  56.6 0.0 reduce-scatter.2.cloned.1.call-update
  56.6 20.6 %reduce-scatter.2.cloned.1.call-done = f32[32,128]{1,0:T(8,128)} async-done(((f32[128,128]{1,0:T(8,128)}), f32[32,128]{1,0:T(8,128)}) %reduce-scatter.2.cloned.1.call-update) | async-done | bytes 16400 | tf_op jit(solution)/shard_map/reduce_scatter | solution.py:91
  77.2 1.3 %multiply_bitcast_fusion = f32[1,32,128]{2,1,0:T(8,128)} fusion(f32[32,128]{1,0:T(8,128)} %reduce-scatter.2.cloned.1.call-done), kind=kLoop, calls=%fused_computation.85 | loop fusion | flops 4096 | bytes 32768 | tf_op jit(solution)/shard_map/broadcast_in_dim | solution.py:93
  (2 shorter events, 0.0 us)
Async XLA Ops:
  6.5 70.6 %reduce-scatter.2.cloned.1.call-start = ((), (), s32[]{:S(2)}) async-start(), calls=%async_computation.1 | async-start | bytes 81920 | tf_op jit(solution)/shard_map/reduce_scatter | solution.py:91
Sparse Core Ops, SparseCore 0:
  56.7 20.4 reduce-scatter.1
where the time goes:
time: 85.8 us; the launch traced here: 85.3 us
  blocking collectives  32.5 us (38%)
  waiting for transfers between devices  20.6 us (24%)
  between operations  14.7 us (17%)
  other arithmetic  14.3 us (17%)
  matrix products  1.87 us (2%)
  local copies, waits for them, and re-layouts  1.37 us (2%)
    all_gather x1, blocking collectives, body(): lax.all_gather(packed, 'facet', axis=0, tiled=True)  32.5 us
    reduce_scatter x1, waiting for transfers between devices, body(): share = lax.psum_scatter(image, 'freq', scatter_dimension=0, tiled=True)  20.6 us
    cos x4, other arithmetic, angle_table(): return (jnp.cos(turns), jnp.sin(turns))  4.38 us
    another operation x2, other arithmetic  3.19 us
    sub x1, other arithmetic, phase_table(): outer_cos = base_cos * coarse_cos - base_sin * coarse_sin  2.21 us
    dot_general x1, matrix products, facet_image(): lax.dot_general(left, right, (((1,), (1,)), ((), ())), preferred_element_...  1.87 us
  transfers between devices with their start and end apart: 1, of which 1 were waited for; matrix products, arithmetic and copies ran while one was open for 0% of the time, Pallas kernels for 0%

commit v1 on v0

v1 whole, which is shorter than its diff:
```python
import functools
import math

import jax
import jax.numpy as jnp
from jax import lax
from jax.experimental import pallas as pl
from jax.experimental.pallas import tpu as pltpu
from jax.sharding import PartitionSpec as P

P_SIZE = 128
IMG = 32768
KEEP = 256
LANES = 128
HALF = P_SIZE // 2
MESH = pl.DeviceIdType.MESH
NT = (((1,), (1,)), ((), ()))


def cos_sin(x):
    q = x * x
    s = jnp.full_like(q, -1.0 / math.factorial(11))
    for order in (9, 7, 5, 3, 1):
        s = s * q + (-1.0) ** (order // 2) / math.factorial(order)
    c = jnp.full_like(q, 1.0 / math.factorial(12))
    for order in (10, 8, 6, 4, 2, 0):
        c = c * q + (-1.0) ** (order // 2) / math.factorial(order)
    return c, s * x


def times(a, b):
    return a[0] * b[0] - a[1] * b[1], a[0] * b[1] + a[1] * b[0]


def square(a):
    return a[0] * a[0] - a[1] * a[1], 2.0 * (a[0] * a[1])


def powers(z, count):
    found = [None, z]
    for k in range(2, count):
        half = found[k // 2]
        found.append(square(half) if k % 2 == 0 else times(found[k // 2 + 1], half))
    return found


def kept_rows(flags):
    blocks, rows = flags.shape
    pieces = [flags[:, j * LANES:(j + 1) * LANES] for j in range(rows // LANES)]
    stacked = jnp.concatenate(pieces, axis=0)
    lower = lax.broadcasted_iota(jnp.int32, (LANES, LANES), 1) <= lax.broadcasted_iota(
        jnp.int32, (LANES, LANES), 0
    )
    inside = lax.dot_general(
        stacked.astype(jnp.bfloat16),
        jnp.where(lower, 1.0, 0.0).astype(jnp.bfloat16),
        NT,
        preferred_element_type=jnp.float32,
    )
    totals = jnp.sum(stacked, axis=1, keepdims=True)
    before = jnp.zeros((blocks, 1), jnp.float32)
    places = []
    for j, piece in enumerate(pieces):
        own = slice(j * blocks, (j + 1) * blocks)
        places.append(jnp.where(piece > 0.5, inside[own] + before - 1.0, -1.0))
        before = before + totals[own]
    return jnp.concatenate(places, axis=1)


def split3(x):
    high = x.astype(jnp.bfloat16).astype(jnp.float32)
    rest = x - high
    middle = rest.astype(jnp.bfloat16).astype(jnp.float32)
    low = rest - middle
    return jnp.concatenate([high, middle, low, jnp.zeros_like(x)], axis=0).astype(jnp.bfloat16)


def kernel(
    n, nf, scale,
    vis_hbm, w_hbm, uv_hbm, flags_hbm, plan_hbm, beam_hbm, facets_hbm,
    out_ref,
    vis, wts, uv, flg, plan, beam, facets,
    buf, fine_c, fine_s, outer_c, outer_s, half_c, half_s, amp, stage, rbuf,
    in_sem, send_sem, recv_sem, rsend_sem, rrecv_sem,
):
    mf = lax.axis_index("freq")
    me = lax.axis_index("facet")
    barrier = pltpu.get_barrier_semaphore()
    loads = [
        pltpu.make_async_copy(src, dst, in_sem.at[k])
        for k, (src, dst) in enumerate(
            [(flags_hbm, flg), (vis_hbm, vis), (w_hbm, wts), (uv_hbm, uv),
             (plan_hbm, plan), (beam_hbm, beam), (facets_hbm, facets)]
        )
    ]
    for load in loads:
        load.start()
    for j in range(1, n):
        pl.semaphore_signal(
            barrier, inc=1, device_id={"facet": lax.rem(me + j, n)}, device_id_type=MESH
        )
    for j in range(1, nf):
        pl.semaphore_signal(
            barrier, inc=1, device_id={"freq": lax.rem(mf + j, nf)}, device_id_type=MESH
        )
    for load in loads:
        load.wait()

    flags = flg[...].astype(jnp.float32)
    place = kept_rows(flags).astype(jnp.int32)
    live = wts[...] * flags
    blocks, rows = flags.shape
    per_block = KEEP // LANES
    four = blocks * per_block
    slot_at = lax.broadcasted_iota(jnp.int32, (KEEP, rows), 0)
    for b in range(blocks):
        chosen = jnp.where(place[b:b + 1, :] == slot_at, 1.0, 0.0).astype(jnp.bfloat16)
        values = jnp.concatenate([vis[b] * live[b:b + 1, :], uv[b].astype(jnp.float32)], axis=0)
        packed = lax.dot_general(split3(values), chosen, NT, preferred_element_type=jnp.float32)
        packed = packed[0:4] + packed[4:8] + packed[8:12]
        for q in range(4):
            for h in range(per_block):
                row = (q % 2) * four + b * per_block + h
                buf[0, q // 2, row:row + 1, :] = packed[q:q + 1, h * LANES:(h + 1) * LANES]

    pl.semaphore_wait(barrier, n - 1 + nf - 1)
    sends = []
    for j in range(1, n):
        sends.append(
            pltpu.make_async_remote_copy(
                src_ref=buf.at[0],
                dst_ref=buf.at[j],
                send_sem=send_sem.at[j],
                recv_sem=recv_sem.at[j],
                device_id={"facet": lax.rem(me + j, n)},
                device_id_type=MESH,
            )
        )
        sends[-1].start()

    tall = 2 * four
    steps = plan.shape[1]
    row_at = lax.broadcasted_iota(jnp.int32, (n * tall, steps), 0)
    source = me - row_at // tall
    source = jnp.where(source < 0, source + n, source)
    block = source * blocks + (row_at % four) // per_block
    gains = jnp.sum(jnp.where(block == plan[...], beam[...] * scale, 0.0), axis=1, keepdims=True)

    high_row = lax.broadcasted_iota(jnp.int32, (tall, LANES), 0) < four
    first = facets[...] * P_SIZE - IMG // 2
    factor = jnp.where(high_row, 2 * first[:, 0:1] + (P_SIZE - 1), 2 * first[:, 1:2])
    sign = jnp.where(high_row, -1.0, 1.0)

    def swap(x):
        return jnp.concatenate([x[:, four:], x[:, :four]], axis=1)

    def tabulate(lo, hi):
        count = hi - lo
        cells = buf[lo:hi, 1]
        half = cos_sin(cells * (math.pi / IMG))
        turns = cells.astype(jnp.int32) * factor[None]
        turns = turns + swap(turns)
        turns = ((turns + IMG) & (2 * IMG - 1)) - IMG
        base = square(cos_sin(turns.astype(jnp.float32) * (math.pi / (2 * IMG))))
        x = buf[lo:hi, 0] * gains[lo * tall:hi * tall].reshape(count, tall, 1)
        amp[lo:hi] = x * base[0] + swap(x) * (base[1] * sign[None])
        half_c[lo:hi] = half[0]
        half_s[lo:hi] = half[1]
        z = square(half)
        one = (jnp.ones_like(z[0]), jnp.zeros_like(z[0]))
        fine = powers(z, 8)
        fine[0] = one
        outer = powers(square(fine[4]), P_SIZE // 8)
        outer[0] = one
        for refs, table in (((fine_c, fine_s), fine), ((outer_c, outer_s), outer)):
            for part in range(2):
                for k, entry in enumerate(table):
                    for i in range(count):
                        at = ((lo + i) * len(table) + k) * tall
                        refs[part][at:at + tall, :] = entry[part][i]

    def image_terms(slot, sums):
        cu, su, re, im = [], [], [], []
        for r in range(four):
            def pick(refs, table_rows, row):
                at = pl.ds(slot * (8 * tall) + row, 8, stride=tall)
                return refs[0][at, :], refs[1][at, :]

            def line(refs, row):
                return refs[0][slot, row:row + 1, :], refs[1][slot, row:row + 1, :]

            def outer_line(k, row):
                at = pl.ds(slot * (16 * tall) + k * tall + row, 1)
                return outer_c[at, :], outer_s[at, :]

            u = times(line((half_c, half_s), r), pick((fine_c, fine_s), 8, r))
            v = times(
                (amp[slot, r:r + 1, :], amp[slot, four + r:four + r + 1, :]),
                pick((fine_c, fine_s), 8, four + r),
            )
            left = [u] + [times(outer_line(k, r), u) for k in range(1, HALF // 8)]
            right = [v] + [times(outer_line(k, four + r), v) for k in range(1, P_SIZE // 8)]
            for kept, table, part in ((cu, left, 0), (su, left, 1), (re, right, 0), (im, right, 1)):
                kept.append(
                    jnp.concatenate([entry[part] for entry in table], axis=0).astype(jnp.bfloat16)
                )
        cu, su, re, im = (jnp.concatenate(kept, axis=1) for kept in (cu, su, re, im))
        return (
            sums[0] + lax.dot_general(cu, re, NT, preferred_element_type=jnp.float32),
            sums[1] + lax.dot_general(su, im, NT, preferred_element_type=jnp.float32),
        )

    zero = jnp.zeros((HALF, P_SIZE), jnp.float32)
    tabulate(0, 1)
    sums = image_terms(0, (zero, zero))
    for j in range(1, n):
        sends[j - 1].wait_recv()
    tabulate(1, n)
    even, odd = lax.fori_loop(1, n, image_terms, sums)

    share = P_SIZE // nf
    for f in range(nf):
        if f < nf // 2:
            at = (nf // 2 - 1 - f) * share
            stage[f] = even[at:at + share] + odd[at:at + share]
        else:
            at = (f - nf // 2) * share
            stage[f] = even[at:at + share] - odd[at:at + share]
    exchanges = []
    for j in range(1, nf):
        to = lax.rem(mf + j, nf)
        exchanges.append(
            pltpu.make_async_remote_copy(
                src_ref=stage.at[to],
                dst_ref=rbuf.at[j],
                send_sem=rsend_sem.at[j],
                recv_sem=rrecv_sem.at[j],
                device_id={"freq": to},
                device_id_type=MESH,
            )
        )
        exchanges[-1].start()
    total = stage[mf]
    for j in range(1, nf):
        exchanges[j - 1].wait_recv()
        total = total + rbuf[j]

    row8 = lax.broadcasted_iota(jnp.int32, (8, P_SIZE), 0)
    mirrored = []
    for k in reversed(range(share // 8)):
        y = pltpu.roll(total[k * 8:(k + 1) * 8], 4, 0)
        y = jnp.where((row8 & 2) != 0, pltpu.roll(y, 2, 0), pltpu.roll(y, 6, 0))
        y = jnp.where((row8 & 1) != 0, pltpu.roll(y, 1, 0), pltpu.roll(y, 7, 0))
        mirrored.append(y)
    mirrored = jnp.concatenate(mirrored, axis=0)
    out_ref[0] = jnp.where(mf < nf // 2, mirrored, total)
    for copy in sends + exchanges:
        copy.wait_send()


def body(n, nf, scale, visibilities, weights, uv_cells, flags, plan, beam, facets):
    blocks, _, rows = visibilities.shape
    four = blocks * (KEEP // LANES)
    tall = 2 * four
    share = P_SIZE // nf
    steps = plan.shape[0]
    f32, i32 = jnp.float32, jnp.int32
    return pl.pallas_call(
        functools.partial(kernel, n, nf, scale),
        out_shape=jax.ShapeDtypeStruct((1, share, P_SIZE), f32),
        in_specs=[pl.BlockSpec(memory_space=pl.ANY)] * 7,
        out_specs=pl.BlockSpec(memory_space=pltpu.VMEM),
        scratch_shapes=[
            pltpu.VMEM((blocks, 2, rows), f32),
            pltpu.VMEM((blocks, rows), f32),
            pltpu.VMEM((blocks, 2, rows), i32),
            pltpu.VMEM((blocks, rows), i32),
            pltpu.VMEM((1, steps), i32),
            pltpu.VMEM((1, steps), f32),
            pltpu.VMEM((1, 2), i32),
            pltpu.VMEM((n, 2, tall, LANES), f32),
            pltpu.VMEM((n * 8 * tall, LANES), f32),
            pltpu.VMEM((n * 8 * tall, LANES), f32),
            pltpu.VMEM((n * 16 * tall, LANES), f32),
            pltpu.VMEM((n * 16 * tall, LANES), f32),
            pltpu.VMEM((n, tall, LANES), f32),
            pltpu.VMEM((n, tall, LANES), f32),
            pltpu.VMEM((n, tall, LANES), f32),
            pltpu.VMEM((nf, share, P_SIZE), f32),
            pltpu.VMEM((nf, share, P_SIZE), f32),
            pltpu.SemaphoreType.DMA((7,)),
            pltpu.SemaphoreType.DMA((n,)),
            pltpu.SemaphoreType.DMA((n,)),
            pltpu.SemaphoreType.DMA((nf,)),
            pltpu.SemaphoreType.DMA((nf,)),
        ],
        compiler_params=pltpu.CompilerParams(
            collective_id=0, has_side_effects=True, vmem_limit_bytes=32 * 1024 * 1024
        ),
        name="facet_image",
    )(visibilities, weights, uv_cells, flags, plan.reshape(1, steps), beam, facets)


def solution(mesh):
    n, nf = mesh.shape["facet"], mesh.shape["freq"]
    in_specs = (
        P("facet", None, "freq"),
        P("facet", "freq"),
        P("facet", None, "freq"),
        P("facet", "freq"),
        P(),
        P("facet", None),
        P("facet", None),
    )
    out_specs = P("facet", "freq", None)

    def whole(visibilities, *others):
        scale = 2.0 / math.sqrt(visibilities.shape[0] * visibilities.shape[2])
        return jax.shard_map(
            functools.partial(body, n, nf, scale),
            mesh=mesh, in_specs=in_specs, out_specs=out_specs, check_vma=False,
        )(visibilities, *others)

    return whole
```

time: 85.8 us -> 18.4 us (0.21)
  blocking collectives: 32.5 us -> 0 us
  waiting for transfers between devices: 20.6 us -> 0 us
  between operations: 14.7 us -> 0.02 us
  other arithmetic: 14.3 us -> 0 us
  Pallas kernels: 0 us -> 14 us
  local copies, waits for them, and re-layouts: 1.37 us -> 4.06 us
  matrix products: 1.87 us -> 0 us
    all_gather x1 -> x0, blocking collectives: 32.5 us -> none  [body(): lax.all_gather(packed, 'facet', axis=0, tiled=True)]
    reduce_scatter x1 -> x0, waiting for transfers between devices: 20.6 us -> none  [body(): share = lax.psum_scatter(image, 'freq', scatter_dimension=0, tiled=True)]
    pallas_call x0 -> x1, Pallas kernels: none -> 14 us  [body(): pl.pallas_call(functools.partial(kernel, n, nf, scale), out_shape=jax.Sha...]
    cos x4 -> x0, other arithmetic: 4.38 us -> none  [angle_table(): return (jnp.cos(turns), jnp.sin(turns))]
    unnamed x0 -> x15, local copies, waits for them, and re-layouts: none -> 4.06 us
    another operation x2 -> x0, other arithmetic: 3.19 us -> none
    sub x1 -> x0, other arithmetic: 2.21 us -> none  [phase_table(): outer_cos = base_cos * coarse_cos - base_sin * coarse_sin]
    dot_general x1 -> x0, matrix products: 1.87 us -> none  [facet_image(): lax.dot_general(left, right, (((1,), (1,)), ((), ())), preferred_element_...]
  transfers between devices with their start and end apart: 1 -> 0, of which waited for: 1 -> 0; matrix products, arithmetic and copies ran while one was open for 0% -> 0% of each run, Pallas kernels for 0% -> 0%
where the time goes in v1:
time: 18.4 us; the launch traced here: 18 us
  Pallas kernels  14 us (76%)
  local copies, waits for them, and re-layouts  4.06 us (22%)
    pallas_call x1, Pallas kernels, body(): pl.pallas_call(functools.partial(kernel, n, nf, scale), out_shape=jax.Sha...  14 us
    unnamed x15, local copies, waits for them, and re-layouts  4.06 us

profile of v1, /device:TPU:0, one launch (start us, length us, event | category | flops | bytes accessed | tf_op | source)
XLA Modules:
  0.0 18.0 jit_solution(153325883217245571)
XLA Ops:
  0.0 0.0 copy-start.6
  0.0 0.0 copy-start.5
  0.0 0.0 copy-start.4
  0.0 0.6 %copy-done.6 = s32[1,2]{1,0:T(1,128)S(1)} copy-done((s32[1,2]{1,0:T(1,128)S(1)}, s32[1,2]{1,0:T(1,128)}, u32[]{:S(2)}) %copy-start.6) | copy-done | bytes 32
  0.7 0.0 copy-done.5
  0.7 0.0 copy-done.4
  0.7 0.0 copy-start
  0.7 0.7 %copy-done = f32[2,2,512]{2,1,0:T(2,128)S(1)} copy-done((f32[2,2,512]{2,1,0:T(2,128)S(1)}, f32[2,2,512]{2,1,0:T(2,128)}, u32[]{:S(2)}) %copy-start) | copy-done | bytes 8216
  1.4 0.0 copy-start.1
  1.4 0.7 %copy-done.1 = s32[2,2,512]{2,1,0:T(2,128)S(1)} copy-done((s32[2,2,512]{2,1,0:T(2,128)S(1)}, s32[2,2,512]{2,1,0:T(2,128)}, u32[]{:S(2)}) %copy-start.1) | copy-done | bytes 8216
  2.1 0.0 copy-start.2
  2.1 0.7 %copy-done.2 = f32[2,512]{1,0:T(2,128)S(1)} copy-done((f32[2,512]{1,0:T(2,128)S(1)}, f32[2,512]{1,0:T(2,128)}, u32[]{:S(2)}) %copy-start.2) | copy-done | bytes 4120
  2.8 0.0 copy-start.3
  2.8 0.7 %copy-done.3 = s32[2,512]{1,0:T(2,128)S(1)} copy-done((s32[2,512]{1,0:T(2,128)S(1)}, s32[2,512]{1,0:T(2,128)}, u32[]{:S(2)}) %copy-start.3) | copy-done | bytes 4120
  3.5 14.0 %facet_image.1 = f32[1,32,128]{2,1,0:T(8,128)S(1)} custom-call(f32[2,2,512]{2,1,0:T(2,128)S(1)} %copy-done, f32[2,512]{1,0:T(2,128)S(1)} %copy-done.2, s32[2,2,512]{2,1,0:T(2,128)S(1)} %copy-done.1, s32[2,512]{1,0:T(2,128)S(1)} %copy-done.3, s32[1,16]{1,0:T(1,128)S(1)} %bitcast.1, f32[1,16]{1,0:T(1,128)S(1)} %copy-done.5, s32[1,2]{1,0:T(1,128)S(1)} %copy-done.6), custom_call_target="tpu_custom_call" | custom-call | tf_op jit(solution)/shard_map/facet_image/pallas_call | solution.py:268
  17.4 0.6 %copy.9 = f32[1,32,128]{2,1,0:T(8,128)} copy(f32[1,32,128]{2,1,0:T(8,128)S(1)} %facet_image.1) | data formatting | bytes 32768
Async XLA Ops:
  0.0 0.7 %copy-start.6 = (s32[1,2]{1,0:T(1,128)S(1)}, s32[1,2]{1,0:T(1,128)}, u32[]{:S(2)}) copy-start(s32[1,2]{1,0:T(1,128)} %facets_hbm.1) | copy-start | bytes 28
  0.0 0.7 %copy-start.5 = (f32[1,16]{1,0:T(1,128)S(1)}, f32[1,16]{1,0:T(1,128)}, u32[]{:S(2)}) copy-start(f32[1,16]{1,0:T(1,128)} %beam_hbm.1) | copy-start | bytes 196
  0.0 0.7 %copy-start.4 = (s32[16]{0:T(128)S(1)}, s32[16]{0:T(128)}, u32[]{:S(2)}) copy-start(s32[16]{0:T(128)} %param.11) | copy-start | bytes 196
  0.7 0.7 %copy-start = (f32[2,2,512]{2,1,0:T(2,128)S(1)}, f32[2,2,512]{2,1,0:T(2,128)}, u32[]{:S(2)}) copy-start(f32[2,2,512]{2,1,0:T(2,128)} %vis_hbm.1) | copy-start | bytes 24580
  1.4 0.7 %copy-start.1 = (s32[2,2,512]{2,1,0:T(2,128)S(1)}, s32[2,2,512]{2,1,0:T(2,128)}, u32[]{:S(2)}) copy-start(s32[2,2,512]{2,1,0:T(2,128)} %uv_hbm.1) | copy-start | bytes 24580
  2.1 0.7 %copy-start.2 = (f32[2,512]{1,0:T(2,128)S(1)}, f32[2,512]{1,0:T(2,128)}, u32[]{:S(2)}) copy-start(f32[2,512]{1,0:T(2,128)} %w_hbm.1) | copy-start | bytes 12292
  2.8 0.7 %copy-start.3 = (s32[2,512]{1,0:T(2,128)S(1)}, s32[2,512]{1,0:T(2,128)}, u32[]{:S(2)}) copy-start(s32[2,512]{1,0:T(2,128)} %flags_hbm.1) | copy-start | bytes 12292

commit v2 on v1

--- a/solution.py
+++ b/solution.py
@@ -216,7 +216,7 @@
     for j in range(1, n):
         sends[j - 1].wait_recv()
     tabulate(1, n)
-    even, odd = lax.fori_loop(1, n, image_terms, sums)
+    even, odd = lax.fori_loop(1, n, image_terms, sums, unroll=n - 1 if n <= 8 else 1)
 
     share = P_SIZE // nf
     for f in range(nf):
@@ -268,7 +268,7 @@
     return pl.pallas_call(
         functools.partial(kernel, n, nf, scale),
         out_shape=jax.ShapeDtypeStruct((1, share, P_SIZE), f32),
-        in_specs=[pl.BlockSpec(memory_space=pl.ANY)] * 7,
+        in_specs=[pl.BlockSpec(memory_space=pltpu.HBM)] * 7,
         out_specs=pl.BlockSpec(memory_space=pltpu.VMEM),
         scratch_shapes=[
             pltpu.VMEM((blocks, 2, rows), f32),
@@ -295,7 +295,7 @@
             pltpu.SemaphoreType.DMA((nf,)),
         ],
         compiler_params=pltpu.CompilerParams(
-            collective_id=0, has_side_effects=True, vmem_limit_bytes=32 * 1024 * 1024
+            collective_id=0, has_side_effects=True, vmem_limit_bytes=62 * 1024 * 1024
         ),
         name="facet_image",
     )(visibilities, weights, uv_cells, flags, plan.reshape(1, steps), beam, facets)

time: 18.4 us -> 15.7 us (0.85)
  local copies, waits for them, and re-layouts: 4.06 us -> 1.32 us
    unnamed x15 -> x1, local copies, waits for them, and re-layouts: 4.06 us -> 1.32 us
where the time goes in v2:
time: 15.7 us; the launch traced here: 15.4 us
  Pallas kernels  14.1 us (90%)
  local copies, waits for them, and re-layouts  1.32 us (8%)
    pallas_call x1, Pallas kernels, body(): pl.pallas_call(functools.partial(kernel, n, nf, scale), out_shape=jax.Sha...  14.1 us
    unnamed x1, local copies, waits for them, and re-layouts  1.32 us

profile of v2, /device:TPU:0, one launch (start us, length us, event | category | flops | bytes accessed | tf_op | source)
XLA Modules:
  0.0 15.4 jit_solution(15673879489504155314)
XLA Ops:
  0.0 14.1 %facet_image.1 = f32[1,32,128]{2,1,0:T(8,128)} custom-call(f32[2,2,512]{2,1,0:T(2,128)} %vis_hbm.1, f32[2,512]{1,0:T(2,128)} %w_hbm.1, s32[2,2,512]{2,1,0:T(2,128)} %uv_hbm.1, s32[2,512]{1,0:T(2,128)} %flags_hbm.1, s32[1,16]{1,0:T(1,128)} %bitcast.1, f32[1,16]{1,0:T(1,128)} %beam_hbm.1, s32[1,2]{1,0:T(1,128)} %facets_hbm.1), custom_call_target="tpu_custom_call" | custom-call | tf_op jit(solution)/shard_map/facet_image/pallas_call | solution.py:268
  14.1 1.3 %copy.9 = f32[1,32,128]{2,1,0:T(8,128)} copy(f32[1,32,128]{2,1,0:T(8,128)} %facet_image.1) | data formatting | bytes 32768

commit v3 on v2

--- a/solution.py
+++ b/solution.py
@@ -13,6 +13,8 @@
 KEEP = 256
 LANES = 128
 HALF = P_SIZE // 2
+FINE = 16
+COARSE = P_SIZE // FINE
 MESH = pl.DeviceIdType.MESH
 NT = (((1,), (1,)), ((), ()))
 
@@ -42,6 +44,20 @@
         half = found[k // 2]
         found.append(square(half) if k % 2 == 0 else times(found[k // 2 + 1], half))
     return found
+
+
+def partner(me, j, n):
+    assert n & (n - 1) == 0
+    found, bit = 0, 1
+    while bit < n:
+        own = lax.rem(me // bit, 2)
+        found = found + bit * (1 - own if j & bit else own)
+        bit *= 2
+    return found
+
+
+def arrival_groups(n):
+    return [(0, 1)] + [(lo, hi) for lo, hi in ((1, n // 2), (n // 2, n)) if lo < hi]
 
 
 def kept_rows(flags):
@@ -95,10 +111,9 @@
     ]
     for load in loads:
         load.start()
-    for j in range(1, n):
-        pl.semaphore_signal(
-            barrier, inc=1, device_id={"facet": lax.rem(me + j, n)}, device_id_type=MESH
-        )
+    peers = [partner(me, j, n) for j in range(n)]
+    for j in reversed(range(1, n)):
+        pl.semaphore_signal(barrier, inc=1, device_id={"facet": peers[j]}, device_id_type=MESH)
     for j in range(1, nf):
         pl.semaphore_signal(
             barrier, inc=1, device_id={"freq": lax.rem(mf + j, nf)}, device_id_type=MESH
@@ -124,27 +139,33 @@
                 buf[0, q // 2, row:row + 1, :] = packed[q:q + 1, h * LANES:(h + 1) * LANES]
 
     pl.semaphore_wait(barrier, n - 1 + nf - 1)
-    sends = []
-    for j in range(1, n):
-        sends.append(
-            pltpu.make_async_remote_copy(
-                src_ref=buf.at[0],
-                dst_ref=buf.at[j],
-                send_sem=send_sem.at[j],
-                recv_sem=recv_sem.at[j],
-                device_id={"facet": lax.rem(me + j, n)},
-                device_id_type=MESH,
-            )
-        )
-        sends[-1].start()
+    sends = [
+        pltpu.make_async_remote_copy(
+            src_ref=buf.at[0],
+            dst_ref=buf.at[j],
+            send_sem=send_sem.at[j],
+            recv_sem=recv_sem.at[j],
+            device_id={"facet": peers[j]},
+            device_id_type=MESH,
+        )
+        for j in range(1, n)
+    ]
+    for send in reversed(sends):
+        send.start()
 
     tall = 2 * four
     steps = plan.shape[1]
-    row_at = lax.broadcasted_iota(jnp.int32, (n * tall, steps), 0)
-    source = me - row_at // tall
-    source = jnp.where(source < 0, source + n, source)
-    block = source * blocks + (row_at % four) // per_block
-    gains = jnp.sum(jnp.where(block == plan[...], beam[...] * scale, 0.0), axis=1, keepdims=True)
+    row_at = lax.broadcasted_iota(jnp.int32, (tall, steps), 0)
+    local = sum(
+        jnp.where((row_at >= h * four + b * per_block) & (row_at < h * four + (b + 1) * per_block), b, 0)
+        for h in range(2) for b in range(1, blocks)
+    )
+    read = plan[...] - local
+    gain = beam[...] * scale
+    gains = [
+        jnp.sum(jnp.where(read == peers[j] * blocks, gain, 0.0), axis=1, keepdims=True)
+        for j in range(n)
+    ]
 
     high_row = lax.broadcasted_iota(jnp.int32, (tall, LANES), 0) < four
     first = facets[...] * P_SIZE - IMG // 2
@@ -162,15 +183,17 @@
         turns = turns + swap(turns)
         turns = ((turns + IMG) & (2 * IMG - 1)) - IMG
         base = square(cos_sin(turns.astype(jnp.float32) * (math.pi / (2 * IMG))))
-        x = buf[lo:hi, 0] * gains[lo * tall:hi * tall].reshape(count, tall, 1)
+        x = buf[lo:hi, 0] * jnp.stack(
+            [jnp.broadcast_to(gains[j], (tall, LANES)) for j in range(lo, hi)]
+        )
         amp[lo:hi] = x * base[0] + swap(x) * (base[1] * sign[None])
         half_c[lo:hi] = half[0]
         half_s[lo:hi] = half[1]
         z = square(half)
         one = (jnp.ones_like(z[0]), jnp.zeros_like(z[0]))
-        fine = powers(z, 8)
+        fine = powers(z, FINE)
         fine[0] = one
-        outer = powers(square(fine[4]), P_SIZE // 8)
+        outer = powers(square(fine[FINE // 2]), COARSE)
         outer[0] = one
         for refs, table in (((fine_c, fine_s), fine), ((outer_c, outer_s), outer)):
             for part in range(2):
@@ -182,24 +205,24 @@
     def image_terms(slot, sums):
         cu, su, re, im = [], [], [], []
         for r in range(four):
-            def pick(refs, table_rows, row):
-                at = pl.ds(slot * (8 * tall) + row, 8, stride=tall)
-                return refs[0][at, :], refs[1][at, :]
+            def pick(row):
+                at = pl.ds(slot * (FINE * tall) + row, FINE, stride=tall)
+                return fine_c[at, :], fine_s[at, :]
 
             def line(refs, row):
                 return refs[0][slot, row:row + 1, :], refs[1][slot, row:row + 1, :]
 
             def outer_line(k, row):
-                at = pl.ds(slot * (16 * tall) + k * tall + row, 1)
+                at = pl.ds(slot * (COARSE * tall) + k * tall + row, 1)
                 return outer_c[at, :], outer_s[at, :]
 
-            u = times(line((half_c, half_s), r), pick((fine_c, fine_s), 8, r))
+            u = times(line((half_c, half_s), r), pick(r))
             v = times(
                 (amp[slot, r:r + 1, :], amp[slot, four + r:four + r + 1, :]),
-                pick((fine_c, fine_s), 8, four + r),
+                pick(four + r),
             )
-            left = [u] + [times(outer_line(k, r), u) for k in range(1, HALF // 8)]
-            right = [v] + [times(outer_line(k, four + r), v) for k in range(1, P_SIZE // 8)]
+            left = [u] + [times(outer_line(k, r), u) for k in range(1, HALF // FINE)]
+            right = [v] + [times(outer_line(k, four + r), v) for k in range(1, COARSE)]
             for kept, table, part in ((cu, left, 0), (su, left, 1), (re, right, 0), (im, right, 1)):
                 kept.append(
                     jnp.concatenate([entry[part] for entry in table], axis=0).astype(jnp.bfloat16)
@@ -210,13 +233,13 @@
             sums[1] + lax.dot_general(su, im, NT, preferred_element_type=jnp.float32),
         )
 
-    zero = jnp.zeros((HALF, P_SIZE), jnp.float32)
-    tabulate(0, 1)
-    sums = image_terms(0, (zero, zero))
-    for j in range(1, n):
-        sends[j - 1].wait_recv()
-    tabulate(1, n)
-    even, odd = lax.fori_loop(1, n, image_terms, sums, unroll=n - 1 if n <= 8 else 1)
+    sums = (jnp.zeros((HALF, P_SIZE), jnp.float32),) * 2
+    for lo, hi in arrival_groups(n):
+        for j in range(max(lo, 1), hi):
+            sends[j - 1].wait_recv()
+        tabulate(lo, hi)
+        sums = lax.fori_loop(lo, hi, image_terms, sums, unroll=hi - lo if hi - lo <= 4 else 1)
+    even, odd = sums
 
     share = P_SIZE // nf
     for f in range(nf):
@@ -267,7 +290,7 @@
     f32, i32 = jnp.float32, jnp.int32
     return pl.pallas_call(
         functools.partial(kernel, n, nf, scale),
-        out_shape=jax.ShapeDtypeStruct((1, share, P_SIZE), f32),
+        out_shape=pltpu.VMEM((1, share, P_SIZE), f32),
         in_specs=[pl.BlockSpec(memory_space=pltpu.HBM)] * 7,
         out_specs=pl.BlockSpec(memory_space=pltpu.VMEM),
         scratch_shapes=[
@@ -279,10 +302,10 @@
             pltpu.VMEM((1, steps), f32),
             pltpu.VMEM((1, 2), i32),
             pltpu.VMEM((n, 2, tall, LANES), f32),
-            pltpu.VMEM((n * 8 * tall, LANES), f32),
-            pltpu.VMEM((n * 8 * tall, LANES), f32),
-            pltpu.VMEM((n * 16 * tall, LANES), f32),
-            pltpu.VMEM((n * 16 * tall, LANES), f32),
+            pltpu.VMEM((n * FINE * tall, LANES), f32),
+            pltpu.VMEM((n * FINE * tall, LANES), f32),
+            pltpu.VMEM((n * COARSE * tall, LANES), f32),
+            pltpu.VMEM((n * COARSE * tall, LANES), f32),
             pltpu.VMEM((n, tall, LANES), f32),
             pltpu.VMEM((n, tall, LANES), f32),
             pltpu.VMEM((n, tall, LANES), f32),

time: 15.7 us -> 13.9 us (0.89)
  Pallas kernels: 14.1 us -> 13.1 us
  local copies, waits for them, and re-layouts: 1.32 us -> 0.61 us
    pallas_call x1, Pallas kernels: 14.1 us -> 13.1 us  [body(): pl.pallas_call(functools.partial(kernel, n, nf, scale), out_shape=pltpu.V...]
    unnamed x1, local copies, waits for them, and re-layouts: 1.32 us -> 0.61 us
where the time goes in v3:
time: 13.9 us; the launch traced here: 13.8 us
  Pallas kernels  13.1 us (94%)
  local copies, waits for them, and re-layouts  0.61 us (4%)
    pallas_call x1, Pallas kernels, body(): pl.pallas_call(functools.partial(kernel, n, nf, scale), out_shape=pltpu.V...  13.1 us
    unnamed x1, local copies, waits for them, and re-layouts  0.61 us

profile of v3, /device:TPU:0, one launch (start us, length us, event | category | flops | bytes accessed | tf_op | source)
XLA Modules:
  0.0 13.8 jit_solution(12854880295834300938)
XLA Ops:
  0.0 13.1 %facet_image.1 = f32[1,32,128]{2,1,0:T(8,128)S(1)} custom-call(f32[2,2,512]{2,1,0:T(2,128)} %vis_hbm.1, f32[2,512]{1,0:T(2,128)} %w_hbm.1, s32[2,2,512]{2,1,0:T(2,128)} %uv_hbm.1, s32[2,512]{1,0:T(2,128)} %flags_hbm.1, s32[1,16]{1,0:T(1,128)} %bitcast.1, f32[1,16]{1,0:T(1,128)} %beam_hbm.1, s32[1,2]{1,0:T(1,128)} %facets_hbm.1), custom_call_target="tpu_custom_call" | custom-call | tf_op jit(solution)/shard_map/facet_image/pallas_call | solution.py:291
  13.2 0.6 %copy.9 = f32[1,32,128]{2,1,0:T(8,128)} copy(f32[1,32,128]{2,1,0:T(8,128)S(1)} %facet_image.1) | data formatting | bytes 32768

commit v4 on v3

--- a/solution.py
+++ b/solution.py
@@ -47,7 +47,7 @@
 
 
 def partner(me, j, n):
-    assert n & (n - 1) == 0
+    assert n >= 4 and n & (n - 1) == 0
     found, bit = 0, 1
     while bit < n:
         own = lax.rem(me // bit, 2)
@@ -57,7 +57,7 @@
 
 
 def arrival_groups(n):
-    return [(0, 1)] + [(lo, hi) for lo, hi in ((1, n // 2), (n // 2, n)) if lo < hi]
+    return [(0, 1)] + [(lo, hi) for lo, hi in ((1, n // 2), (n // 2, n - n // 4), (n - n // 4, n))]
 
 
 def kept_rows(flags):
@@ -118,7 +118,7 @@
         pl.semaphore_signal(
             barrier, inc=1, device_id={"freq": lax.rem(mf + j, nf)}, device_id_type=MESH
         )
-    for load in loads:
+    for load in loads[:4]:
         load.wait()
 
     flags = flg[...].astype(jnp.float32)
@@ -152,6 +152,9 @@
     ]
     for send in reversed(sends):
         send.start()
+
+    for load in loads[4:]:
+        load.wait()
 
     tall = 2 * four
     steps = plan.shape[1]

time: 13.9 us -> 14 us (level)
  no operation moved by 1% of the time
where the time goes in v4:
time: 14 us; the launch traced here: 13.8 us
  Pallas kernels  13.2 us (94%)
  local copies, waits for them, and re-layouts  0.61 us (4%)
    pallas_call x1, Pallas kernels, body(): pl.pallas_call(functools.partial(kernel, n, nf, scale), out_shape=pltpu.V...  13.2 us
    unnamed x1, local copies, waits for them, and re-layouts  0.61 us

profile of v4, /device:TPU:0, one launch (start us, length us, event | category | flops | bytes accessed | tf_op | source)
XLA Modules:
  0.0 13.8 jit_solution(7365121757305573448)
XLA Ops:
  0.0 13.2 %facet_image.1 = f32[1,32,128]{2,1,0:T(8,128)S(1)} custom-call(f32[2,2,512]{2,1,0:T(2,128)} %vis_hbm.1, f32[2,512]{1,0:T(2,128)} %w_hbm.1, s32[2,2,512]{2,1,0:T(2,128)} %uv_hbm.1, s32[2,512]{1,0:T(2,128)} %flags_hbm.1, s32[1,16]{1,0:T(1,128)} %bitcast.1, f32[1,16]{1,0:T(1,128)} %beam_hbm.1, s32[1,2]{1,0:T(1,128)} %facets_hbm.1), custom_call_target="tpu_custom_call" | custom-call | tf_op jit(solution)/shard_map/facet_image/pallas_call | solution.py:294
  13.2 0.6 %copy.9 = f32[1,32,128]{2,1,0:T(8,128)} copy(f32[1,32,128]{2,1,0:T(8,128)S(1)} %facet_image.1) | data formatting | bytes 32768

commit v5 on v4

--- a/solution.py
+++ b/solution.py
@@ -57,7 +57,7 @@
 
 
 def arrival_groups(n):
-    return [(0, 1)] + [(lo, hi) for lo, hi in ((1, n // 2), (n // 2, n - n // 4), (n - n // 4, n))]
+    return [(0, 1)] + [(lo, hi) for lo, hi in ((1, n // 2), (n // 2, n))]
 
 
 def kept_rows(flags):
@@ -88,7 +88,10 @@
     rest = x - high
     middle = rest.astype(jnp.bfloat16).astype(jnp.float32)
     low = rest - middle
-    return jnp.concatenate([high, middle, low, jnp.zeros_like(x)], axis=0).astype(jnp.bfloat16)
+    pieces = [high, middle, low]
+    if x.shape[0] % 16:
+        pieces.append(jnp.zeros_like(x))
+    return jnp.concatenate(pieces, axis=0).astype(jnp.bfloat16)
 
 
 def kernel(
@@ -172,7 +175,7 @@
 
     high_row = lax.broadcasted_iota(jnp.int32, (tall, LANES), 0) < four
     first = facets[...] * P_SIZE - IMG // 2
-    factor = jnp.where(high_row, 2 * first[:, 0:1] + (P_SIZE - 1), 2 * first[:, 1:2])
+    factor = jnp.where(high_row, 2 * first[:, 0:1], 2 * first[:, 1:2] + (P_SIZE - 1))
     sign = jnp.where(high_row, -1.0, 1.0)
 
     def swap(x):
@@ -206,7 +209,7 @@
                         refs[part][at:at + tall, :] = entry[part][i]
 
     def image_terms(slot, sums):
-        cu, su, re, im = [], [], [], []
+        re, im, cv, sv = [], [], [], []
         for r in range(four):
             def pick(row):
                 at = pl.ds(slot * (FINE * tall) + row, FINE, stride=tall)
@@ -219,24 +222,23 @@
                 at = pl.ds(slot * (COARSE * tall) + k * tall + row, 1)
                 return outer_c[at, :], outer_s[at, :]
 
-            u = times(line((half_c, half_s), r), pick(r))
-            v = times(
-                (amp[slot, r:r + 1, :], amp[slot, four + r:four + r + 1, :]),
-                pick(four + r),
+            u = times(
+                (amp[slot, r:r + 1, :], amp[slot, four + r:four + r + 1, :]), pick(r)
             )
-            left = [u] + [times(outer_line(k, r), u) for k in range(1, HALF // FINE)]
-            right = [v] + [times(outer_line(k, four + r), v) for k in range(1, COARSE)]
-            for kept, table, part in ((cu, left, 0), (su, left, 1), (re, right, 0), (im, right, 1)):
+            v = times(line((half_c, half_s), four + r), pick(four + r))
+            left = [u] + [times(outer_line(k, r), u) for k in range(1, COARSE)]
+            right = [v] + [times(outer_line(k, four + r), v) for k in range(1, HALF // FINE)]
+            for kept, table, part in ((re, left, 0), (im, left, 1), (cv, right, 0), (sv, right, 1)):
                 kept.append(
                     jnp.concatenate([entry[part] for entry in table], axis=0).astype(jnp.bfloat16)
                 )
-        cu, su, re, im = (jnp.concatenate(kept, axis=1) for kept in (cu, su, re, im))
+        re, im, cv, sv = (jnp.concatenate(kept, axis=1) for kept in (re, im, cv, sv))
         return (
-            sums[0] + lax.dot_general(cu, re, NT, preferred_element_type=jnp.float32),
-            sums[1] + lax.dot_general(su, im, NT, preferred_element_type=jnp.float32),
-        )
-
-    sums = (jnp.zeros((HALF, P_SIZE), jnp.float32),) * 2
+            sums[0] + lax.dot_general(re, cv, NT, preferred_element_type=jnp.float32),
+            sums[1] + lax.dot_general(im, sv, NT, preferred_element_type=jnp.float32),
+        )
+
+    sums = (jnp.zeros((P_SIZE, HALF), jnp.float32),) * 2
     for lo, hi in arrival_groups(n):
         for j in range(max(lo, 1), hi):
             sends[j - 1].wait_recv()
@@ -245,13 +247,7 @@
     even, odd = sums
 
     share = P_SIZE // nf
-    for f in range(nf):
-        if f < nf // 2:
-            at = (nf // 2 - 1 - f) * share
-            stage[f] = even[at:at + share] + odd[at:at + share]
-        else:
-            at = (f - nf // 2) * share
-            stage[f] = even[at:at + share] - odd[at:at + share]
+    stage[...] = jnp.concatenate([even - odd, even + odd], axis=1).reshape(nf, share, P_SIZE)
     exchanges = []
     for j in range(1, nf):
         to = lax.rem(mf + j, nf)
@@ -271,15 +267,14 @@
         exchanges[j - 1].wait_recv()
         total = total + rbuf[j]
 
-    row8 = lax.broadcasted_iota(jnp.int32, (8, P_SIZE), 0)
-    mirrored = []
-    for k in reversed(range(share // 8)):
-        y = pltpu.roll(total[k * 8:(k + 1) * 8], 4, 0)
-        y = jnp.where((row8 & 2) != 0, pltpu.roll(y, 2, 0), pltpu.roll(y, 6, 0))
-        y = jnp.where((row8 & 1) != 0, pltpu.roll(y, 1, 0), pltpu.roll(y, 7, 0))
-        mirrored.append(y)
-    mirrored = jnp.concatenate(mirrored, axis=0)
-    out_ref[0] = jnp.where(mf < nf // 2, mirrored, total)
+    goal = lax.broadcasted_iota(jnp.int32, (P_SIZE, P_SIZE), 0)
+    origin = jnp.where(goal < HALF, P_SIZE - 1 - goal, goal - HALF)
+    moves = origin == lax.broadcasted_iota(jnp.int32, (P_SIZE, P_SIZE), 1)
+    moved = lax.dot_general(
+        split3(total), jnp.where(moves, 1.0, 0.0).astype(jnp.bfloat16), NT,
+        preferred_element_type=jnp.float32,
+    )
+    out_ref[0] = moved[:share] + moved[share:2 * share] + moved[2 * share:3 * share]
     for copy in sends + exchanges:
         copy.wait_send()
 

time: 14 us -> 14.2 us (1.014)
  Pallas kernels: 13.2 us -> 13.4 us
    pallas_call x1, Pallas kernels: 13.2 us -> 13.4 us  [body(): pl.pallas_call(functools.partial(kernel, n, nf, scale), out_shape=pltpu.V...]
where the time goes in v5:
time: 14.2 us; the launch traced here: 14 us
  Pallas kernels  13.4 us (94%)
  local copies, waits for them, and re-layouts  0.61 us (4%)
    pallas_call x1, Pallas kernels, body(): pl.pallas_call(functools.partial(kernel, n, nf, scale), out_shape=pltpu.V...  13.4 us
    unnamed x1, local copies, waits for them, and re-layouts  0.61 us

profile of v5, /device:TPU:0, one launch (start us, length us, event | category | flops | bytes accessed | tf_op | source)
XLA Modules:
  0.0 14.0 jit_solution(14496595405205485792)
XLA Ops:
  0.0 13.4 %facet_image.1 = f32[1,32,128]{2,1,0:T(8,128)S(1)} custom-call(f32[2,2,512]{2,1,0:T(2,128)} %vis_hbm.1, f32[2,512]{1,0:T(2,128)} %w_hbm.1, s32[2,2,512]{2,1,0:T(2,128)} %uv_hbm.1, s32[2,512]{1,0:T(2,128)} %flags_hbm.1, s32[1,16]{1,0:T(1,128)} %bitcast.1, f32[1,16]{1,0:T(1,128)} %beam_hbm.1, s32[1,2]{1,0:T(1,128)} %facets_hbm.1), custom_call_target="tpu_custom_call" | custom-call | tf_op jit(solution)/shard_map/facet_image/pallas_call | solution.py:289
  13.4 0.6 %copy.9 = f32[1,32,128]{2,1,0:T(8,128)} copy(f32[1,32,128]{2,1,0:T(8,128)S(1)} %facet_image.1) | data formatting | bytes 32768

commit v6 on v3

--- a/solution.py
+++ b/solution.py
@@ -13,8 +13,7 @@
 KEEP = 256
 LANES = 128
 HALF = P_SIZE // 2
-FINE = 16
-COARSE = P_SIZE // FINE
+FINE = 8
 MESH = pl.DeviceIdType.MESH
 NT = (((1,), (1,)), ((), ()))
 
@@ -96,7 +95,7 @@
     vis_hbm, w_hbm, uv_hbm, flags_hbm, plan_hbm, beam_hbm, facets_hbm,
     out_ref,
     vis, wts, uv, flg, plan, beam, facets,
-    buf, fine_c, fine_s, outer_c, outer_s, half_c, half_s, amp, stage, rbuf,
+    buf, fine_c, fine_s, step_c, step_s, half_c, half_s, amp, stage, rbuf,
     in_sem, send_sem, recv_sem, rsend_sem, rrecv_sem,
 ):
     mf = lax.axis_index("freq")
@@ -109,16 +108,16 @@
              (plan_hbm, plan), (beam_hbm, beam), (facets_hbm, facets)]
         )
     ]
-    for load in loads:
-        load.start()
+    for j in range(1, nf):
+        pl.semaphore_signal(
+            barrier, inc=1, device_id={"freq": lax.rem(mf + j, nf)}, device_id_type=MESH
+        )
     peers = [partner(me, j, n) for j in range(n)]
     for j in reversed(range(1, n)):
         pl.semaphore_signal(barrier, inc=1, device_id={"facet": peers[j]}, device_id_type=MESH)
-    for j in range(1, nf):
-        pl.semaphore_signal(
-            barrier, inc=1, device_id={"freq": lax.rem(mf + j, nf)}, device_id_type=MESH
-        )
     for load in loads:
+        load.start()
+    for load in loads[:4]:
         load.wait()
 
     flags = flg[...].astype(jnp.float32)
@@ -153,6 +152,9 @@
     for send in reversed(sends):
         send.start()
 
+    for load in loads[4:]:
+        load.wait()
+
     tall = 2 * four
     steps = plan.shape[1]
     row_at = lax.broadcasted_iota(jnp.int32, (tall, steps), 0)
@@ -193,14 +195,12 @@
         one = (jnp.ones_like(z[0]), jnp.zeros_like(z[0]))
         fine = powers(z, FINE)
         fine[0] = one
-        outer = powers(square(fine[FINE // 2]), COARSE)
-        outer[0] = one
-        for refs, table in (((fine_c, fine_s), fine), ((outer_c, outer_s), outer)):
-            for part in range(2):
-                for k, entry in enumerate(table):
-                    for i in range(count):
-                        at = ((lo + i) * len(table) + k) * tall
-                        refs[part][at:at + tall, :] = entry[part][i]
+        step_c[lo:hi], step_s[lo:hi] = square(fine[FINE // 2])
+        for ref, part in ((fine_c, 0), (fine_s, 1)):
+            for k, entry in enumerate(fine):
+                for i in range(count):
+                    at = ((lo + i) * FINE + k) * tall
+                    ref[at:at + tall, :] = entry[part][i]
 
     def image_terms(slot, sums):
         cu, su, re, im = [], [], [], []
@@ -212,17 +212,23 @@
             def line(refs, row):
                 return refs[0][slot, row:row + 1, :], refs[1][slot, row:row + 1, :]
 
-            def outer_line(k, row):
-                at = pl.ds(slot * (COARSE * tall) + k * tall + row, 1)
-                return outer_c[at, :], outer_s[at, :]
+            def climb(start, row, rows_at):
+                step = line((step_c, step_s), row)
+                double = jnp.broadcast_to(step[0] + step[0], (FINE, LANES))
+                table = [start, times(step, start)]
+                while len(table) * FINE < rows_at:
+                    table.append(
+                        tuple(double * now - past for past, now in zip(table[-2], table[-1]))
+                    )
+                return table
 
             u = times(line((half_c, half_s), r), pick(r))
             v = times(
                 (amp[slot, r:r + 1, :], amp[slot, four + r:four + r + 1, :]),
                 pick(four + r),
             )
-            left = [u] + [times(outer_line(k, r), u) for k in range(1, HALF // FINE)]
-            right = [v] + [times(outer_line(k, four + r), v) for k in range(1, COARSE)]
+            left = climb(u, r, HALF)
+            right = climb(v, four + r, P_SIZE)
             for kept, table, part in ((cu, left, 0), (su, left, 1), (re, right, 0), (im, right, 1)):
                 kept.append(
                     jnp.concatenate([entry[part] for entry in table], axis=0).astype(jnp.bfloat16)
@@ -304,8 +310,8 @@
             pltpu.VMEM((n, 2, tall, LANES), f32),
             pltpu.VMEM((n * FINE * tall, LANES), f32),
             pltpu.VMEM((n * FINE * tall, LANES), f32),
-            pltpu.VMEM((n * COARSE * tall, LANES), f32),
-            pltpu.VMEM((n * COARSE * tall, LANES), f32),
+            pltpu.VMEM((n, tall, LANES), f32),
+            pltpu.VMEM((n, tall, LANES), f32),
             pltpu.VMEM((n, tall, LANES), f32),
             pltpu.VMEM((n, tall, LANES), f32),
             pltpu.VMEM((n, tall, LANES), f32),

time: 13.9 us -> 13.8 us (level)
    pallas_call x1, Pallas kernels: 13.1 us -> 13 us  [body(): pl.pallas_call(functools.partial(kernel, n, nf, scale), out_shape=pltpu.V...]
where the time goes in v6:
time: 13.8 us; the launch traced here: 13.6 us
  Pallas kernels  13 us (94%)
  local copies, waits for them, and re-layouts  0.61 us (4%)
    pallas_call x1, Pallas kernels, body(): pl.pallas_call(functools.partial(kernel, n, nf, scale), out_shape=pltpu.V...  13 us
    unnamed x1, local copies, waits for them, and re-layouts  0.61 us

profile of v6, /device:TPU:0, one launch (start us, length us, event | category | flops | bytes accessed | tf_op | source)
XLA Modules:
  0.0 13.6 jit_solution(615322034445849727)
XLA Ops:
  0.0 13.0 %facet_image.1 = f32[1,32,128]{2,1,0:T(8,128)S(1)} custom-call(f32[2,2,512]{2,1,0:T(2,128)} %vis_hbm.1, f32[2,512]{1,0:T(2,128)} %w_hbm.1, s32[2,2,512]{2,1,0:T(2,128)} %uv_hbm.1, s32[2,512]{1,0:T(2,128)} %flags_hbm.1, s32[1,16]{1,0:T(1,128)} %bitcast.1, f32[1,16]{1,0:T(1,128)} %beam_hbm.1, s32[1,2]{1,0:T(1,128)} %facets_hbm.1), custom_call_target="tpu_custom_call" | custom-call | tf_op jit(solution)/shard_map/facet_image/pallas_call | solution.py:297
  13.0 0.6 %copy.9 = f32[1,32,128]{2,1,0:T(8,128)} copy(f32[1,32,128]{2,1,0:T(8,128)S(1)} %facet_image.1) | data formatting | bytes 32768

commit v7 on v6

--- a/solution.py
+++ b/solution.py
@@ -56,7 +56,7 @@
 
 
 def arrival_groups(n):
-    return [(0, 1)] + [(lo, hi) for lo, hi in ((1, n // 2), (n // 2, n)) if lo < hi]
+    return [(0, 1), (1, n)]
 
 
 def kept_rows(flags):
@@ -108,20 +108,22 @@
              (plan_hbm, plan), (beam_hbm, beam), (facets_hbm, facets)]
         )
     ]
-    for j in range(1, nf):
+    for load in loads[:4]:
+        load.start()
+    for j in reversed(range(1, nf)):
         pl.semaphore_signal(
-            barrier, inc=1, device_id={"freq": lax.rem(mf + j, nf)}, device_id_type=MESH
+            barrier, inc=1, device_id={"freq": partner(mf, j, nf)}, device_id_type=MESH
         )
     peers = [partner(me, j, n) for j in range(n)]
     for j in reversed(range(1, n)):
         pl.semaphore_signal(barrier, inc=1, device_id={"facet": peers[j]}, device_id_type=MESH)
-    for load in loads:
+    for load in loads[4:]:
         load.start()
-    for load in loads[:4]:
-        load.wait()
-
+    loads[0].wait()
     flags = flg[...].astype(jnp.float32)
     place = kept_rows(flags).astype(jnp.int32)
+    for load in loads[1:4]:
+        load.wait()
     live = wts[...] * flags
     blocks, rows = flags.shape
     per_block = KEEP // LANES
@@ -244,7 +246,7 @@
         for j in range(max(lo, 1), hi):
             sends[j - 1].wait_recv()
         tabulate(lo, hi)
-        sums = lax.fori_loop(lo, hi, image_terms, sums, unroll=hi - lo if hi - lo <= 4 else 1)
+        sums = lax.fori_loop(lo, hi, image_terms, sums, unroll=hi - lo if hi - lo <= 8 else 1)
     even, odd = sums
 
     share = P_SIZE // nf
@@ -256,8 +258,8 @@
             at = (f - nf // 2) * share
             stage[f] = even[at:at + share] - odd[at:at + share]
     exchanges = []
-    for j in range(1, nf):
-        to = lax.rem(mf + j, nf)
+    for j in reversed(range(1, nf)):
+        to = partner(mf, j, nf)
         exchanges.append(
             pltpu.make_async_remote_copy(
                 src_ref=stage.at[to],
@@ -270,8 +272,9 @@
         )
         exchanges[-1].start()
     total = stage[mf]
+    for exchange in exchanges:
+        exchange.wait_recv()
     for j in range(1, nf):
-        exchanges[j - 1].wait_recv()
         total = total + rbuf[j]
 
     row8 = lax.broadcasted_iota(jnp.int32, (8, P_SIZE), 0)

time: 13.8 us -> 14.3 us (1.036)
  Pallas kernels: 13 us -> 13.5 us
    pallas_call x1, Pallas kernels: 13 us -> 13.5 us  [body(): pl.pallas_call(functools.partial(kernel, n, nf, scale), out_shape=pltpu.V...]
where the time goes in v7:
time: 14.3 us; the launch traced here: 14.1 us
  Pallas kernels  13.5 us (94%)
  local copies, waits for them, and re-layouts  0.61 us (4%)
    pallas_call x1, Pallas kernels, body(): pl.pallas_call(functools.partial(kernel, n, nf, scale), out_shape=pltpu.V...  13.5 us
    unnamed x1, local copies, waits for them, and re-layouts  0.61 us

profile of v7, /device:TPU:0, one launch (start us, length us, event | category | flops | bytes accessed | tf_op | source)
XLA Modules:
  0.0 14.1 jit_solution(15904822727799737621)
XLA Ops:
  0.0 13.5 %facet_image.1 = f32[1,32,128]{2,1,0:T(8,128)S(1)} custom-call(f32[2,2,512]{2,1,0:T(2,128)} %vis_hbm.1, f32[2,512]{1,0:T(2,128)} %w_hbm.1, s32[2,2,512]{2,1,0:T(2,128)} %uv_hbm.1, s32[2,512]{1,0:T(2,128)} %flags_hbm.1, s32[1,16]{1,0:T(1,128)} %bitcast.1, f32[1,16]{1,0:T(1,128)} %beam_hbm.1, s32[1,2]{1,0:T(1,128)} %facets_hbm.1), custom_call_target="tpu_custom_call" | custom-call | tf_op jit(solution)/shard_map/facet_image/pallas_call | solution.py:300
  13.5 0.6 %copy.9 = f32[1,32,128]{2,1,0:T(8,128)} copy(f32[1,32,128]{2,1,0:T(8,128)S(1)} %facet_image.1) | data formatting | bytes 32768

commit v8 on v7

--- a/solution.py
+++ b/solution.py
@@ -56,7 +56,7 @@
 
 
 def arrival_groups(n):
-    return [(0, 1), (1, n)]
+    return [(0, 1), (1, n // 2), (n // 2, n - n // 4), (n - n // 4, n)]
 
 
 def kept_rows(flags):

time: 14.3 us -> 14 us (0.979)
  Pallas kernels: 13.5 us -> 13.2 us
    pallas_call x1, Pallas kernels: 13.5 us -> 13.2 us  [body(): pl.pallas_call(functools.partial(kernel, n, nf, scale), out_shape=pltpu.V...]
where the time goes in v8:
time: 14 us; the launch traced here: 13.8 us
  Pallas kernels  13.2 us (94%)
  local copies, waits for them, and re-layouts  0.61 us (4%)
    pallas_call x1, Pallas kernels, body(): pl.pallas_call(functools.partial(kernel, n, nf, scale), out_shape=pltpu.V...  13.2 us
    unnamed x1, local copies, waits for them, and re-layouts  0.61 us

profile of v8, /device:TPU:0, one launch (start us, length us, event | category | flops | bytes accessed | tf_op | source)
XLA Modules:
  0.0 13.8 jit_solution(14197079852245345256)
XLA Ops:
  0.0 13.2 %facet_image.1 = f32[1,32,128]{2,1,0:T(8,128)S(1)} custom-call(f32[2,2,512]{2,1,0:T(2,128)} %vis_hbm.1, f32[2,512]{1,0:T(2,128)} %w_hbm.1, s32[2,2,512]{2,1,0:T(2,128)} %uv_hbm.1, s32[2,512]{1,0:T(2,128)} %flags_hbm.1, s32[1,16]{1,0:T(1,128)} %bitcast.1, f32[1,16]{1,0:T(1,128)} %beam_hbm.1, s32[1,2]{1,0:T(1,128)} %facets_hbm.1), custom_call_target="tpu_custom_call" | custom-call | tf_op jit(solution)/shard_map/facet_image/pallas_call | solution.py:300
  13.2 0.6 %copy.9 = f32[1,32,128]{2,1,0:T(8,128)} copy(f32[1,32,128]{2,1,0:T(8,128)S(1)} %facet_image.1) | data formatting | bytes 32768

commit v9 on v8

--- a/solution.py
+++ b/solution.py
@@ -235,11 +235,10 @@
                 kept.append(
                     jnp.concatenate([entry[part] for entry in table], axis=0).astype(jnp.bfloat16)
                 )
-        cu, su, re, im = (jnp.concatenate(kept, axis=1) for kept in (cu, su, re, im))
-        return (
-            sums[0] + lax.dot_general(cu, re, NT, preferred_element_type=jnp.float32),
-            sums[1] + lax.dot_general(su, im, NT, preferred_element_type=jnp.float32),
-        )
+        left = jnp.concatenate([jnp.concatenate(kept, axis=1) for kept in (cu, su)], axis=0)
+        right = jnp.concatenate([jnp.concatenate(kept, axis=1) for kept in (re, im)], axis=0)
+        term = lax.dot_general(left, right, NT, preferred_element_type=jnp.float32)
+        return sums[0] + term[:HALF, :P_SIZE], sums[1] + term[HALF:, P_SIZE:]
 
     sums = (jnp.zeros((HALF, P_SIZE), jnp.float32),) * 2
     for lo, hi in arrival_groups(n):

time: 14 us -> 14.3 us (1.021)
  Pallas kernels: 13.2 us -> 13.5 us
    pallas_call x1, Pallas kernels: 13.2 us -> 13.5 us  [body(): pl.pallas_call(functools.partial(kernel, n, nf, scale), out_shape=pltpu.V...]
where the time goes in v9:
time: 14.3 us; the launch traced here: 14.1 us
  Pallas kernels  13.5 us (94%)
  local copies, waits for them, and re-layouts  0.61 us (4%)
    pallas_call x1, Pallas kernels, body(): pl.pallas_call(functools.partial(kernel, n, nf, scale), out_shape=pltpu.V...  13.5 us
    unnamed x1, local copies, waits for them, and re-layouts  0.61 us

profile of v9, /device:TPU:0, one launch (start us, length us, event | category | flops | bytes accessed | tf_op | source)
XLA Modules:
  0.0 14.1 jit_solution(18296539161092467548)
XLA Ops:
  0.0 13.5 %facet_image.1 = f32[1,32,128]{2,1,0:T(8,128)S(1)} custom-call(f32[2,2,512]{2,1,0:T(2,128)} %vis_hbm.1, f32[2,512]{1,0:T(2,128)} %w_hbm.1, s32[2,2,512]{2,1,0:T(2,128)} %uv_hbm.1, s32[2,512]{1,0:T(2,128)} %flags_hbm.1, s32[1,16]{1,0:T(1,128)} %bitcast.1, f32[1,16]{1,0:T(1,128)} %beam_hbm.1, s32[1,2]{1,0:T(1,128)} %facets_hbm.1), custom_call_target="tpu_custom_call" | custom-call | tf_op jit(solution)/shard_map/facet_image/pallas_call | solution.py:299
  13.5 0.6 %copy.9 = f32[1,32,128]{2,1,0:T(8,128)} copy(f32[1,32,128]{2,1,0:T(8,128)S(1)} %facet_image.1) | data formatting | bytes 32768

commit v10 on v8

--- a/solution.py
+++ b/solution.py
@@ -20,12 +20,18 @@
 
 def cos_sin(x):
     q = x * x
-    s = jnp.full_like(q, -1.0 / math.factorial(11))
-    for order in (9, 7, 5, 3, 1):
-        s = s * q + (-1.0) ** (order // 2) / math.factorial(order)
-    c = jnp.full_like(q, 1.0 / math.factorial(12))
-    for order in (10, 8, 6, 4, 2, 0):
-        c = c * q + (-1.0) ** (order // 2) / math.factorial(order)
+    q2 = q * q
+    q4 = q2 * q2
+
+    def pairwise(first):
+        terms = [(-1.0) ** (k // 2) / math.factorial(k) for k in range(first, 14, 2)]
+        low = (terms[0] + terms[1] * q) + (terms[2] + terms[3] * q) * q2
+        high = terms[4] + terms[5] * q
+        if len(terms) > 6:
+            high = high + terms[6] * q2
+        return low + high * q4
+
+    c, s = pairwise(0), pairwise(1)
     return c, s * x
 
 
@@ -56,7 +62,7 @@
 
 
 def arrival_groups(n):
-    return [(0, 1), (1, n // 2), (n // 2, n - n // 4), (n - n // 4, n)]
+    return [(0, 1), (1, n // 2), (n // 2, n - n // 4), (n - n // 4, n - 1), (n - 1, n)]
 
 
 def kept_rows(flags):

time: 14 us -> 14 us (level)
  no operation moved by 1% of the time
where the time goes in v10:
time: 14 us; the launch traced here: 13.8 us
  Pallas kernels  13.2 us (94%)
  local copies, waits for them, and re-layouts  0.61 us (4%)
    pallas_call x1, Pallas kernels, body(): pl.pallas_call(functools.partial(kernel, n, nf, scale), out_shape=pltpu.V...  13.2 us
    unnamed x1, local copies, waits for them, and re-layouts  0.61 us

profile of v10, /device:TPU:0, one launch (start us, length us, event | category | flops | bytes accessed | tf_op | source)
XLA Modules:
  0.0 13.8 jit_solution(6476856071738594067)
XLA Ops:
  0.0 13.2 %facet_image.1 = f32[1,32,128]{2,1,0:T(8,128)S(1)} custom-call(f32[2,2,512]{2,1,0:T(2,128)} %vis_hbm.1, f32[2,512]{1,0:T(2,128)} %w_hbm.1, s32[2,2,512]{2,1,0:T(2,128)} %uv_hbm.1, s32[2,512]{1,0:T(2,128)} %flags_hbm.1, s32[1,16]{1,0:T(1,128)} %bitcast.1, f32[1,16]{1,0:T(1,128)} %beam_hbm.1, s32[1,2]{1,0:T(1,128)} %facets_hbm.1), custom_call_target="tpu_custom_call" | custom-call | tf_op jit(solution)/shard_map/facet_image/pallas_call | solution.py:306
  13.2 0.6 %copy.9 = f32[1,32,128]{2,1,0:T(8,128)} copy(f32[1,32,128]{2,1,0:T(8,128)S(1)} %facet_image.1) | data formatting | bytes 32768

commit v11 on v8

--- a/solution.py
+++ b/solution.py
@@ -42,6 +42,14 @@
     for k in range(2, count):
         half = found[k // 2]
         found.append(square(half) if k % 2 == 0 else times(found[k // 2 + 1], half))
+    return found
+
+
+def exclusive(a, b, n):
+    found, bit = 0, 1
+    while bit < n:
+        found = found + bit * lax.rem(a // bit + b // bit, 2)
+        bit *= 2
     return found
 
 
@@ -140,19 +148,21 @@
                 buf[0, q // 2, row:row + 1, :] = packed[q:q + 1, h * LANES:(h + 1) * LANES]
 
     pl.semaphore_wait(barrier, n - 1 + nf - 1)
-    sends = [
-        pltpu.make_async_remote_copy(
+    def to_peer(slot, device, k):
+        return pltpu.make_async_remote_copy(
             src_ref=buf.at[0],
-            dst_ref=buf.at[j],
-            send_sem=send_sem.at[j],
-            recv_sem=recv_sem.at[j],
-            device_id={"facet": peers[j]},
+            dst_ref=buf.at[slot],
+            send_sem=send_sem.at[k],
+            recv_sem=recv_sem.at[slot],
+            device_id={"facet": device},
             device_id_type=MESH,
         )
-        for j in range(1, n)
-    ]
-    for send in reversed(sends):
-        send.start()
+
+    sends = []
+    for k in range(n - 1):
+        device = k + jnp.where(me <= k, 1, 0)
+        sends.append(to_peer(exclusive(me, device, n), device, k))
+        sends[-1].start()
 
     for load in loads[4:]:
         load.wait()
@@ -244,7 +254,7 @@
     sums = (jnp.zeros((HALF, P_SIZE), jnp.float32),) * 2
     for lo, hi in arrival_groups(n):
         for j in range(max(lo, 1), hi):
-            sends[j - 1].wait_recv()
+            to_peer(j, peers[j], 0).wait_recv()
         tabulate(lo, hi)
         sums = lax.fori_loop(lo, hi, image_terms, sums, unroll=hi - lo if hi - lo <= 8 else 1)
     even, odd = sums

time: 14 us -> 13.8 us (0.986)
  Pallas kernels: 13.2 us -> 13 us
    pallas_call x1, Pallas kernels: 13.2 us -> 13 us  [body(): pl.pallas_call(functools.partial(kernel, n, nf, scale), out_shape=pltpu.V...]
where the time goes in v11:
time: 13.8 us; the launch traced here: 13.6 us
  Pallas kernels  13 us (94%)
  local copies, waits for them, and re-layouts  0.61 us (4%)
    pallas_call x1, Pallas kernels, body(): pl.pallas_call(functools.partial(kernel, n, nf, scale), out_shape=pltpu.V...  13 us
    unnamed x1, local copies, waits for them, and re-layouts  0.61 us

profile of v11, /device:TPU:0, one launch (start us, length us, event | category | flops | bytes accessed | tf_op | source)
XLA Modules:
  0.0 13.6 jit_solution(17951628466956832350)
XLA Ops:
  0.0 13.0 %facet_image.1 = f32[1,32,128]{2,1,0:T(8,128)S(1)} custom-call(f32[2,2,512]{2,1,0:T(2,128)} %vis_hbm.1, f32[2,512]{1,0:T(2,128)} %w_hbm.1, s32[2,2,512]{2,1,0:T(2,128)} %uv_hbm.1, s32[2,512]{1,0:T(2,128)} %flags_hbm.1, s32[1,16]{1,0:T(1,128)} %bitcast.1, f32[1,16]{1,0:T(1,128)} %beam_hbm.1, s32[1,2]{1,0:T(1,128)} %facets_hbm.1), custom_call_target="tpu_custom_call" | custom-call | tf_op jit(solution)/shard_map/facet_image/pallas_call | solution.py:310
  13.0 0.6 %copy.9 = f32[1,32,128]{2,1,0:T(8,128)} copy(f32[1,32,128]{2,1,0:T(8,128)S(1)} %facet_image.1) | data formatting | bytes 32768
